TPU v7x, 32 devices: a whole 2x2x4 slice. The times are simulated.
32 devices in a mesh: req: 4 (over y, x), grp: 8 (over z, core).
Axes of the slice: x: 2, y: 2, z: 4, core: 2. Of those that a mesh axis runs over, the one named last changes fastest.
Arguments:
- residual: bfloat16 [4, 8, 128, 4096], P('req', 'grp'), may hold values from -64 to 64
- suffix_proj: bfloat16 [4, 8, 3, 128, 4096], P('req', 'grp'), may hold values from -256 to 256
- prefix_cache: bfloat16 [4, 8, 2, 128, 4096], P('req', 'grp'), may hold values from -8 to 8
- owner_req: int32 [8], replicated, may hold values from 0 to 3, as said below
- lengths: int32 [4, 8], P('req', 'grp'), may hold values from 8 to 128, as said below
- norm_gain: float32 [4096], replicated, may hold values from 0.1 to 1.9
- up_weight: bfloat16 [12288, 4096], P('grp'), may hold values from -0.09375 to 0.09375
- down_weight: bfloat16 [12288, 4096], P('grp'), may hold values from -0.0546875 to 0.0546875
Outputs:
- output: bfloat16 [4, 8, 128, 4096], P('req', 'grp')
Inputs may be any that keep to these rules, and one draw needn't show every extreme that they name: owner_req[g] is the req index whose cache block holds group g's prefix. The first lengths[r, g] of the 128 slots of a request are live; in every req index one request fills all 128 slots.
All inputs are finite; a program needn't handle non-finite values.
Results may differ from a plain program's by a relative error of at most 0.014.
Values may be sent and summed in bfloat16 or wider, within the bound.
A program may use at most 128 MiB of HBM per device.

v0:
```python
import math

import jax
import jax.numpy as jnp
from jax import lax
from jax.sharding import PartitionSpec as P

HEADS = 32


NORM_EPS = 1e-05


def from_root(value, axis, source):
    kept = jnp.where(lax.axis_index(axis) == source, value, 0).astype(value.dtype)
    return lax.psum(kept, axis)


def head_slopes(head_count):
    return jnp.exp2(-8.0 * jnp.arange(1, head_count + 1, dtype=jnp.float32) / head_count)


def attend(queries, key_rows, value_rows, key_pos, query_pos, causal):
    head_size = queries.shape[2]
    scores = jnp.einsum("qhe,khe->hqk", queries, key_rows, preferred_element_type=jnp.float32)
    scores = scores * (1.0 / math.sqrt(head_size))
    offsets = (key_pos[None, :] - query_pos[:, None]).astype(jnp.float32)
    scores = scores + head_slopes(queries.shape[1])[:, None, None] * offsets[None, :, :]
    if causal:
        scores = jnp.where((key_pos[None, :] <= query_pos[:, None])[None], scores, -jnp.inf)
    row_max = jnp.max(scores, axis=2)
    weights = jnp.exp(scores - row_max[:, :, None])
    row_total = jnp.sum(weights, axis=2)
    context = jnp.einsum(
        "hqk,khe->qhe", weights.astype(jnp.bfloat16), value_rows, preferred_element_type=jnp.float32
    )
    return (row_max, row_total, context)


def merge_parts(first, second):
    joint_max = jnp.maximum(first[0], second[0])
    first_scale = jnp.exp(first[0] - joint_max)
    second_scale = jnp.exp(second[0] - joint_max)
    numer = first[2] * first_scale.T[:, :, None] + second[2] * second_scale.T[:, :, None]
    denom = first[1] * first_scale + second[1] * second_scale
    merged = numer / denom.T[:, :, None]
    return merged.reshape(merged.shape[0], merged.shape[1] * merged.shape[2])


def layer_norm(state, norm_gain):
    values = state.astype(jnp.float32)
    center = values - jnp.mean(values, axis=-1, keepdims=True)
    spread = jnp.mean(center * center, axis=-1, keepdims=True)
    return (center * lax.rsqrt(spread + NORM_EPS) * norm_gain).astype(jnp.bfloat16)


def body(
    residual, suffix_proj, prefix_cache, owner_req, lengths, norm_gain, up_weight, down_weight
):
    slot_count = residual.shape[2]
    feature_count = residual.shape[3]
    prefix_count = prefix_cache.shape[3]
    head_count = HEADS
    head_size = feature_count // head_count
    block = suffix_proj[0, 0].reshape(3, slot_count, head_count, head_size)
    query_pos = prefix_count + jnp.arange(slot_count, dtype=jnp.int32)
    prefix_pos = jnp.arange(prefix_count, dtype=jnp.int32)
    group_index = lax.axis_index("grp")
    owner_index = lax.dynamic_index_in_dim(owner_req, group_index, 0, keepdims=False)
    cached = from_root(prefix_cache[0, 0], "req", owner_index)
    cached = cached.reshape(2, prefix_count, head_count, head_size)
    first = attend(block[0], cached[0], cached[1], prefix_pos, query_pos, False)
    second = attend(block[0], block[1], block[2], query_pos, query_pos, True)
    context = merge_parts(first, second)
    states = (residual[0, 0].astype(jnp.float32) + context).astype(jnp.bfloat16)
    normed = layer_norm(states, norm_gain)
    preactivation = lax.dot_general(
        lax.all_gather(normed, "grp", axis=0, tiled=True),
        up_weight,
        (((1,), (1,)), ((), ())),
        preferred_element_type=jnp.float32,
    )
    hidden = jax.nn.gelu(preactivation, approximate=False).astype(jnp.bfloat16)
    partial_term = jnp.dot(hidden, down_weight, preferred_element_type=jnp.float32).astype(
        jnp.bfloat16
    )
    mlp_sum = lax.psum_scatter(
        lax.optimization_barrier(partial_term).astype(jnp.float32).astype(jnp.bfloat16),
        "grp",
        scatter_dimension=0,
        tiled=True,
    ).astype(jnp.float32)
    live = jnp.arange(slot_count, dtype=jnp.int32) < lengths[0, 0]
    combined = states.astype(jnp.float32) + mlp_sum
    output = jnp.where(live[:, None], combined, 0.0).astype(jnp.bfloat16)
    return output[None, None]


def solution(mesh):
    placed = (
        P("req", "grp", None, None),
        P("req", "grp", None, None, None),
        P("req", "grp", None, None, None),
        P(),
        P("req", "grp"),
        P(),
        P("grp", None),
        P("grp", None),
    )
    return jax.shard_map(
        body, mesh=mesh, in_specs=placed, out_specs=P("req", "grp", None, None), check_vma=False
    )
```

profile of v0, /device:TPU:0, one launch (start us, length us, event | category | flops | bytes accessed | tf_op | source)
XLA Modules:
  0.0 326.2 jit_solution(6801374428552046400)
XLA Ops:
  6.5 3.1 copy.16
  9.7 1.2 dynamic_slice.4
  11.6 1.4 select_bitcast_fusion
  13.1 3.6 %fusion.96 = (bf16[1,1,1,128,4096]{4,3,2,1,0:T(8,128)(2,1)}, bf16[1,1,1,128,4096]{4,3,2,1,0:T(8,128)(2,1)}, bf16[1,1,1,128,4096]{4,3,2,1,0:T(8,128)(2,1)S(1)}) fusion(bf16[1,1,3,128,4096]{4,3,2,1,0:T(8,128)(2,1)} %param.9), kind=kLoop, calls=%fused_computation.126 | loop fusion | bytes 6291456 | tf_op jit(solution)/shard_map/slice | solution.py:73
  16.7 1.6 copy.35
  18.3 2.3 copy.36
  20.6 1.3 copy.25
  21.9 1.6 copy.28
  23.6 0.1 broadcast_compare_fusion
  23.7 3.4 %fusion.99 = (f32[32,128]{1,0:T(8,128)S(1)}, f32[32,128,128]{1,2,0:T(8,128)}) fusion(f32[128,128]{0,1:T(8,128)S(1)} %get-tuple-element.15, f32[32]{0:T(128)S(1)} %multiply_exponential_fusion, bf16[128,32,128]{0,2,1:T(8,128)(2,1)S(1)} %bitcast.61, bf16[128,32,128]{0,2,1:T(8,128)(2,1)} %bitcast.68, pred[128,128]{0,1:T(8,128)(4,1)S(1)} %broadcast_compare_fusion), kind=kOutput, calls=%fused_computation.129 | convolution fusion | flops 136835072 | bytes 4292736 | tf_op jit(solution)/shard_map/qhe,khe->hqk/dot_general | solution.py:25
  27.1 58.4 %all-reduce.2.cloned.1.call-done = bf16[2,128,4096]{1,2,0:T(8,128)(2,1)} async-done(((bf16[2,128,4096]{1,2,0:T(8,128)(2,1)}), bf16[2,128,4096]{1,2,0:T(8,128)(2,1)}) %all-reduce.2.cloned.1.call-update) | async-done | bytes 2097168 | tf_op jit(solution)/shard_map/psum | solution.py:16
  85.5 1.8 fusion.97
  87.4 0.7 fusion.98
  88.1 0.5 fusion.56
  88.6 1.0 fusion.51
  89.7 2.5 convert_reduce_fusion
  92.2 1.9 copy.27
  94.1 1.8 fusion.47
  95.9 1.4 fusion.43
  97.4 82.2 %all-gather.2.cloned.1.call-done = bf16[1024,4096]{1,0:T(8,128)(2,1)} async-done(((bf16[128,4096]{1,0:T(8,128)(2,1)}), bf16[1024,4096]{1,0:T(8,128)(2,1)}) %all-gather.2.cloned.1.call-update) | async-done | bytes 8388624 | tf_op jit(solution)/shard_map/all_gather | solution.py:78
  179.6 16.8 %fusion.100 = f32[1024,1536]{1,0:T(8,128)S(1)} fusion(bf16[1024,4096]{1,0:T(8,128)(2,1)} %all-gather.2.cloned.1.call-done, bf16[1536,4096]{1,0:T(8,128)(2,1)} %param.14), kind=kOutput, calls=%fused_computation.130 | convolution fusion | flops 12884901888 | bytes 27262976 | tf_op jit(solution)/shard_map/dot_general | solution.py:77
  196.4 32.3 %convolution_convert_fusion = bf16[1024,4096]{1,0:T(8,128)(2,1)} fusion(bf16[1536,4096]{1,0:T(8,128)(2,1)} %param.15, f32[1024,1536]{1,0:T(8,128)S(1)} %fusion.100), kind=kOutput, calls=%fused_computation.1 | convolution fusion | flops 12991332352 | bytes 27262976 | tf_op jit(solution)/shard_map/dot_general | solution.py:84
  229.4 87.6 %reduce-scatter.2.cloned.1.call-done = bf16[128,4096]{1,0:T(8,128)(2,1)} async-done(((bf16[1024,4096]{1,0:T(8,128)(2,1)}), bf16[128,4096]{1,0:T(8,128)(2,1)}) %reduce-scatter.2.cloned.1.call-update) | async-done | bytes 1048592 | tf_op jit(solution)/shard_map/reduce_scatter | solution.py:87
  317.1 2.6 fusion.58
  (23 shorter events, 0.3 us)
Async XLA Ops:
  6.5 79.0 %all-reduce.2.cloned.1.call-start = ((), (), s32[]{:S(2)}) async-start(), calls=%async_computation.1 | async-start | bytes 4194304 | tf_op jit(solution)/shard_map/psum | solution.py:16
  13.0 8.9 %copy-start = (bf16[1,1,128,4096]{3,2,1,0:T(8,128)(2,1)S(1)}, bf16[1,1,128,4096]{3,2,1,0:T(8,128)(2,1)}, u32[]{:S(2)}) copy-start(bf16[1,1,128,4096]{3,2,1,0:T(8,128)(2,1)} %param.8) | copy-start | bytes 3145732
  13.0 166.5 %all-gather.2.cloned.1.call-start = ((), (), s32[]{:S(2)}) async-start(), calls=%async_computation.2 | async-start | bytes 9437184 | tf_op jit(solution)/shard_map/all_gather | solution.py:78
  85.5 3.1 copy-start.2
  87.4 2.3 copy-start.1
  87.4 2.3 copy-start.3
  89.7 6.3 %copy-start.4 = (f32[4096]{0:T(1024)S(1)}, f32[4096]{0:T(1024)}, u32[]{:S(2)}) copy-start(f32[4096]{0:T(1024)} %param.13) | copy-start | bytes 49156
  97.4 219.7 %reduce-scatter.2.cloned.1.call-start = ((), (), s32[]{:S(2)}) async-start(), calls=%async_computation.3 | async-start | bytes 9437184 | tf_op jit(solution)/shard_map/reduce_scatter | solution.py:87
Sparse Core Ops, SparseCore 0:
  13.2 72.3 all-reduce.1
  97.5 82.0 all-gather.1
  228.9 88.1 reduce-scatter.1
where the time goes:
time: 327 us; the launch traced here: 326 us
  waiting for transfers between devices  228 us (70%)
  matrix products  56.2 us (17%)
  local copies, waits for them, and re-layouts  18.6 us (6%)
  between operations  14.6 us (4%)
  other arithmetic  8.51 us (3%)
    reduce_scatter x1, waiting for transfers between devices, body(): lax.psum_scatter(lax.optimization_barrier(partial_term).astype(jnp.float3...  87.6 us
    all_gather x1, waiting for transfers between devices, body(): lax.all_gather(normed, 'grp', axis=0, tiled=True)  82.2 us
    psum x1, waiting for transfers between devices, from_root(): return lax.psum(kept, axis)  58.4 us
    dot_general x1, matrix products, body(): jnp.dot(hidden, down_weight, preferred_element_type=jnp.float32)  32.3 us
    dot_general x1, matrix products, body(): lax.dot_general(lax.all_gather(normed, 'grp', axis=0, tiled=True), up_wei...  16.8 us
    unnamed x13, local copies, waits for them, and re-layouts  7.11 us
  transfers between devices with their start and end apart: 3, of which 3 were waited for; matrix products, arithmetic and copies ran while one was open for 4% of the time, Pallas kernels for 0%

commit v1 on v0

--- a/solution.py
+++ b/solution.py
@@ -1,8 +1,11 @@
+import functools
 import math
 
 import jax
 import jax.numpy as jnp
 from jax import lax
+from jax.experimental import pallas as pl
+from jax.experimental.pallas import tpu as pltpu
 from jax.sharding import PartitionSpec as P
 
 HEADS = 32
@@ -11,9 +14,21 @@
 NORM_EPS = 1e-05
 
 
-def from_root(value, axis, source):
-    kept = jnp.where(lax.axis_index(axis) == source, value, 0).astype(value.dtype)
-    return lax.psum(kept, axis)
+def swap_halves(half, bits, req_size, owner_index):
+    mine = lax.axis_index("req")
+    for bit in bits:
+        pairs = [(r, r ^ (1 << bit)) for r in range(req_size)]
+        other = lax.ppermute(half, "req", pairs)
+        same = ((mine >> bit) & 1) == ((owner_index >> bit) & 1)
+        half = jnp.where(same, half, other)
+    return half
+
+
+def from_owner(block, req_size, owner_index):
+    bits = list(range(req_size.bit_length() - 1))
+    keys = swap_halves(block[0], bits, req_size, owner_index)
+    values = swap_halves(block[1], bits[::-1], req_size, owner_index)
+    return keys, values
 
 
 def head_slopes(head_count):
@@ -54,7 +69,333 @@
     return (center * lax.rsqrt(spread + NORM_EPS) * norm_gain).astype(jnp.bfloat16)
 
 
+MESH = pl.DeviceIdType.MESH
+AG_PARTS = 2
+RS_PARTS = 4
+UP_TILE = 512
+DOWN_TILE = 512
+
+
+def mlp_kernel(
+    chips, normed_hbm, state_ref, up_hbm, down_hbm, out_ref,
+    xg, upv, dnv, hid, part, sib, line,
+    wsem, ag_recv, ag_send, sib_send, sib_recv, rs_send, rs_recv,
+):
+    rows = xg.shape[2]
+    width = xg.shape[3]
+    units = upv.shape[0]
+    ag_rows = rows // AG_PARTS
+    rs_rows = rows // RS_PARTS
+    me = lax.axis_index("grp")
+    z = me // 2
+    c = me % 2
+    twin = z * 2 + 1 - c
+    has_left = z > 0
+    has_right = z < chips - 1
+
+    up_copy = pltpu.make_async_copy(up_hbm, upv, wsem.at[0])
+    down_copy = pltpu.make_async_copy(down_hbm, dnv, wsem.at[1])
+    own_copy = pltpu.make_async_copy(normed_hbm, xg.at[z, c], wsem.at[2])
+    own_copy.start()
+    up_copy.start()
+    down_copy.start()
+
+    barrier = pltpu.get_barrier_semaphore()
+    pl.semaphore_signal(barrier, inc=1, device_id={"grp": twin}, device_id_type=MESH)
+
+    @pl.when(has_left)
+    def _():
+        pl.semaphore_signal(barrier, inc=1, device_id={"grp": me - 2}, device_id_type=MESH)
+
+    @pl.when(has_right)
+    def _():
+        pl.semaphore_signal(barrier, inc=1, device_id={"grp": me + 2}, device_id_type=MESH)
+
+    @pl.when(jnp.logical_and(has_left, has_right))
+    def _():
+        pl.semaphore_wait(barrier, 3)
+
+    @pl.when(jnp.logical_not(jnp.logical_and(has_left, has_right)))
+    def _():
+        pl.semaphore_wait(barrier, 2)
+
+    own_copy.wait()
+
+    def ag_copy(zb, cc, s, way, target):
+        piece = xg.at[zb, cc, pl.ds(s * ag_rows, ag_rows)]
+        return pltpu.make_async_remote_copy(
+            src_ref=piece, dst_ref=piece,
+            send_sem=ag_send.at[way, zb, s], recv_sem=ag_recv.at[zb, cc, s],
+            device_id={"grp": target}, device_id_type=MESH,
+        )
+
+    def sib_copy(zb):
+        return pltpu.make_async_remote_copy(
+            src_ref=part.at[zb, 1 - c], dst_ref=sib.at[zb],
+            send_sem=sib_send.at[zb], recv_sem=sib_recv.at[zb],
+            device_id={"grp": twin}, device_id_type=MESH,
+        )
+
+    def rs_copy(zb, slot, q, target):
+        span = pl.ds(q * rs_rows, rs_rows)
+        return pltpu.make_async_remote_copy(
+            src_ref=part.at[zb, c, span], dst_ref=line.at[slot, span],
+            send_sem=rs_send.at[zb, q], recv_sem=rs_recv.at[slot, q],
+            device_id={"grp": target}, device_id_type=MESH,
+        )
+
+    for s in range(AG_PARTS):
+        @pl.when(has_right)
+        def _():
+            ag_copy(z, c, s, 0, me + 2).start()
+
+        @pl.when(has_left)
+        def _():
+            ag_copy(z, c, s, 1, me - 2).start()
+
+        ag_copy(z, c, s, 2, twin).start()
+
+    up_copy.wait()
+    down_copy.wait()
+
+    def compute(zb):
+        for s in range(AG_PARTS):
+            ag_copy(zb, 1 - c, s, 2, twin).wait_recv()
+
+        def up_step(j, carry):
+            cols = pl.ds(pl.multiple_of(j * UP_TILE, UP_TILE), UP_TILE)
+            pre = lax.dot_general(
+                xg[zb].reshape(2 * rows, width), upv[cols, :],
+                (((1,), (1,)), ((), ())), preferred_element_type=jnp.float32,
+            )
+            act = 0.5 * pre * (1.0 + lax.erf(pre * math.sqrt(0.5)))
+            hid[:, cols] = act.astype(jnp.bfloat16)
+            return carry
+
+        lax.fori_loop(0, units // UP_TILE, up_step, 0)
+
+        def down_step(j, carry):
+            cols = pl.ds(pl.multiple_of(j * DOWN_TILE, DOWN_TILE), DOWN_TILE)
+            term = jnp.dot(hid[...], dnv[:, cols], preferred_element_type=jnp.float32)
+            part[zb, :, :, cols] = term.astype(jnp.bfloat16).reshape(2, rows, DOWN_TILE)
+            return carry
+
+        lax.fori_loop(0, width // DOWN_TILE, down_step, 0)
+        sib_copy(zb).start()
+
+    def add_line(zb, q, with_line):
+        span = pl.ds(q * rs_rows, rs_rows)
+        total = part[zb, c, span].astype(jnp.float32) + sib[zb, span].astype(jnp.float32)
+        if with_line:
+            total = total + line[zb, span].astype(jnp.float32)
+        part[zb, c, span] = total.astype(jnp.bfloat16)
+
+    def step(d, carry):
+        low, high = z - d, z + d
+        for s in range(AG_PARTS):
+            @pl.when(jnp.logical_and(d > 0, low >= 0))
+            def _():
+                ag_copy(low, c, s, 0, twin).wait_recv()
+
+                @pl.when(has_right)
+                def _():
+                    ag_copy(low, c, s, 0, me + 2).start()
+
+                ag_copy(low, c, s, 2, twin).start()
+
+            @pl.when(jnp.logical_and(d > 0, high < chips))
+            def _():
+                ag_copy(high, c, s, 1, twin).wait_recv()
+
+                @pl.when(has_left)
+                def _():
+                    ag_copy(high, c, s, 1, me - 2).start()
+
+                ag_copy(high, c, s, 2, twin).start()
+
+        def side_step(side, inner):
+            zb = z - d + 2 * d * side
+
+            @pl.when(jnp.logical_and(jnp.logical_and(zb >= 0, zb < chips), d + 1 > side))
+            def _():
+                compute(zb)
+
+            return inner
+
+        lax.fori_loop(0, 2, side_step, 0)
+
+        to_right = d
+        to_left = chips - 1 - d
+        goes_right = z < to_right
+        goes_left = z > to_left
+
+        @pl.when(goes_right)
+        def _():
+            sib_copy(to_right).wait_recv()
+
+        @pl.when(goes_left)
+        def _():
+            sib_copy(to_left).wait_recv()
+
+        for q in range(RS_PARTS):
+            @pl.when(goes_right)
+            def _():
+                @pl.when(has_left)
+                def _():
+                    rs_copy(to_right, to_right, q, twin).wait_recv()
+                    add_line(to_right, q, True)
+
+                @pl.when(jnp.logical_not(has_left))
+                def _():
+                    add_line(to_right, q, False)
+
+                rs_copy(to_right, to_right, q, me + 2).start()
+
+            @pl.when(goes_left)
+            def _():
+                @pl.when(has_right)
+                def _():
+                    rs_copy(to_left, to_left, q, twin).wait_recv()
+                    add_line(to_left, q, True)
+
+                @pl.when(jnp.logical_not(has_right))
+                def _():
+                    add_line(to_left, q, False)
+
+                @pl.when(z - 1 == to_left)
+                def _():
+                    rs_copy(to_left, chips, q, me - 2).start()
+
+                @pl.when(z - 1 > to_left)
+                def _():
+                    rs_copy(to_left, to_left, q, me - 2).start()
+
+        return carry
+
+    lax.fori_loop(0, chips, step, 0)
+
+    sib_copy(z).wait_recv()
+    for q in range(RS_PARTS):
+        span = pl.ds(q * rs_rows, rs_rows)
+
+        @pl.when(has_left)
+        def _():
+            rs_copy(z, z, q, twin).wait_recv()
+
+        @pl.when(has_right)
+        def _():
+            rs_copy(z, chips, q, twin).wait_recv()
+
+        def finish(slots):
+            total = part[z, c, span].astype(jnp.float32) + sib[z, span].astype(jnp.float32)
+            for slot in slots:
+                total = total + line[slot, span].astype(jnp.float32)
+            total = total + state_ref[span].astype(jnp.float32)
+            out_ref[span] = total.astype(jnp.bfloat16)
+
+        @pl.when(jnp.logical_and(has_left, has_right))
+        def _():
+            finish([z, chips])
+
+        @pl.when(jnp.logical_not(has_left))
+        def _():
+            finish([chips])
+
+        @pl.when(jnp.logical_not(has_right))
+        def _():
+            finish([z])
+
+    def drain(zb, carry):
+        for s in range(AG_PARTS):
+            @pl.when(jnp.logical_and(has_right, zb <= z))
+            def _():
+                ag_copy(zb, c, s, 0, twin).wait_send()
+
+            @pl.when(jnp.logical_and(has_left, zb >= z))
+            def _():
+                ag_copy(zb, c, s, 1, twin).wait_send()
+
+            ag_copy(zb, c, s, 2, twin).wait_send()
+        sib_copy(zb).wait_send()
+        for q in range(RS_PARTS):
+            @pl.when(zb != z)
+            def _():
+                rs_copy(zb, zb, q, twin).wait_send()
+        return carry
+
+    lax.fori_loop(0, chips, drain, 0)
+
+
+def mlp_bytes(grp_size, rows, width, units):
+    chips = grp_size // 2
+    blocks = 2 * chips + 2 * chips + chips + chips + 1 + 4
+    return 2 * width * (blocks * rows + 2 * units) + 4 * rows * units
+
+
+VMEM_LIMIT = 60 * 1024 * 1024
+
+
+def mlp_fused(grp_size, normed, states, up_weight, down_weight):
+    chips = grp_size // 2
+    rows, width = normed.shape
+    units = up_weight.shape[0]
+    bf16 = jnp.bfloat16
+    dma = pltpu.SemaphoreType.DMA
+    total_rows = rows * grp_size
+    return pl.pallas_call(
+        functools.partial(mlp_kernel, chips),
+        out_shape=jax.ShapeDtypeStruct((rows, width), bf16),
+        in_specs=[
+            pl.BlockSpec(memory_space=pl.ANY),
+            pl.BlockSpec(memory_space=pltpu.VMEM),
+            pl.BlockSpec(memory_space=pl.ANY),
+            pl.BlockSpec(memory_space=pl.ANY),
+        ],
+        out_specs=pl.BlockSpec(memory_space=pltpu.VMEM),
+        scratch_shapes=[
+            pltpu.VMEM((chips, 2, rows, width), bf16),
+            pltpu.VMEM((units, width), bf16),
+            pltpu.VMEM((units, width), bf16),
+            pltpu.VMEM((2 * rows, units), bf16),
+            pltpu.VMEM((chips, 2, rows, width), bf16),
+            pltpu.VMEM((chips, rows, width), bf16),
+            pltpu.VMEM((chips + 1, rows, width), bf16),
+            dma((3,)),
+            dma((chips, 2, AG_PARTS)),
+            dma((3, chips, AG_PARTS)),
+            dma((chips,)),
+            dma((chips,)),
+            dma((chips, RS_PARTS)),
+            dma((chips + 1, RS_PARTS)),
+        ],
+        compiler_params=pltpu.CompilerParams(
+            collective_id=0, has_side_effects=True, vmem_limit_bytes=VMEM_LIMIT
+        ),
+        cost_estimate=pl.CostEstimate(
+            flops=4 * total_rows * width * units,
+            bytes_accessed=4 * units * width,
+            transcendentals=total_rows * units,
+        ),
+    )(normed, states, up_weight, down_weight)
+
+
+def mlp_plain(normed, states, up_weight, down_weight):
+    preactivation = lax.dot_general(
+        lax.all_gather(normed, "grp", axis=0, tiled=True),
+        up_weight,
+        (((1,), (1,)), ((), ())),
+        preferred_element_type=jnp.float32,
+    )
+    hidden = jax.nn.gelu(preactivation, approximate=False).astype(jnp.bfloat16)
+    partial_term = jnp.dot(hidden, down_weight, preferred_element_type=jnp.float32).astype(
+        jnp.bfloat16
+    )
+    mlp_sum = lax.psum_scatter(partial_term, "grp", scatter_dimension=0, tiled=True)
+    return (states.astype(jnp.float32) + mlp_sum.astype(jnp.float32)).astype(jnp.bfloat16)
+
+
 def body(
+    req_size, grp_size,
     residual, suffix_proj, prefix_cache, owner_req, lengths, norm_gain, up_weight, down_weight
 ):
     slot_count = residual.shape[2]
@@ -67,32 +408,19 @@
     prefix_pos = jnp.arange(prefix_count, dtype=jnp.int32)
     group_index = lax.axis_index("grp")
     owner_index = lax.dynamic_index_in_dim(owner_req, group_index, 0, keepdims=False)
-    cached = from_root(prefix_cache[0, 0], "req", owner_index)
-    cached = cached.reshape(2, prefix_count, head_count, head_size)
+    cached = from_owner(prefix_cache[0, 0], req_size, owner_index)
+    cached = [half.reshape(prefix_count, head_count, head_size) for half in cached]
     first = attend(block[0], cached[0], cached[1], prefix_pos, query_pos, False)
     second = attend(block[0], block[1], block[2], query_pos, query_pos, True)
     context = merge_parts(first, second)
     states = (residual[0, 0].astype(jnp.float32) + context).astype(jnp.bfloat16)
     normed = layer_norm(states, norm_gain)
-    preactivation = lax.dot_general(
-        lax.all_gather(normed, "grp", axis=0, tiled=True),
-        up_weight,
-        (((1,), (1,)), ((), ())),
-        preferred_element_type=jnp.float32,
-    )
-    hidden = jax.nn.gelu(preactivation, approximate=False).astype(jnp.bfloat16)
-    partial_term = jnp.dot(hidden, down_weight, preferred_element_type=jnp.float32).astype(
-        jnp.bfloat16
-    )
-    mlp_sum = lax.psum_scatter(
-        lax.optimization_barrier(partial_term).astype(jnp.float32).astype(jnp.bfloat16),
-        "grp",
-        scatter_dimension=0,
-        tiled=True,
-    ).astype(jnp.float32)
+    if mlp_bytes(grp_size, slot_count, feature_count, up_weight.shape[0]) <= VMEM_LIMIT * 15 // 16:
+        combined = mlp_fused(grp_size, normed, states, up_weight, down_weight)
+    else:
+        combined = mlp_plain(normed, states, up_weight, down_weight)
     live = jnp.arange(slot_count, dtype=jnp.int32) < lengths[0, 0]
-    combined = states.astype(jnp.float32) + mlp_sum
-    output = jnp.where(live[:, None], combined, 0.0).astype(jnp.bfloat16)
+    output = jnp.where(live[:, None], combined, jnp.zeros_like(combined))
     return output[None, None]
 
 
@@ -108,5 +436,6 @@
         P("grp", None),
     )
     return jax.shard_map(
-        body, mesh=mesh, in_specs=placed, out_specs=P("req", "grp", None, None), check_vma=False
+        functools.partial(body, mesh.shape["req"], mesh.shape["grp"]),
+        mesh=mesh, in_specs=placed, out_specs=P("req", "grp", None, None), check_vma=False
     )

time: 327 us -> 231 us (0.71)
  waiting for transfers between devices: 228 us -> 40 us
  Pallas kernels: 0 us -> 146 us
  matrix products: 56.2 us -> 8.84 us
  between operations: 14.6 us -> 2.15 us
  starting transfers between devices: 0.09 us -> 6.45 us
    pallas_call x0 -> x1, Pallas kernels: none -> 146 us  [mlp_fused(): pl.pallas_call(functools.partial(mlp_kernel, chips), out_shape=jax.ShapeD...]
    reduce_scatter x1 -> x0, waiting for transfers between devices: 87.6 us -> none  [body(): lax.psum_scatter(lax.optimization_barrier(partial_term).astype(jnp.float3...]
    all_gather x1 -> x0, waiting for transfers between devices: 82.2 us -> none  [body(): lax.all_gather(normed, 'grp', axis=0, tiled=True)]
    psum x1 -> x0, waiting for transfers between devices: 58.4 us -> none  [from_root(): return lax.psum(kept, axis)]
    dot_general x2 -> x0, matrix products: 49.2 us -> none  [the longest x1 32.3 us: body(): jnp.dot(hidden, down_weight, preferred_element_type=jnp.float32)]
    ppermute x0 -> x4, waiting for transfers between devices: none -> 40 us  [swap_halves(): other = lax.ppermute(half, 'req', pairs)]
    ppermute x0 -> x4, starting transfers between devices: none -> 6.45 us  [swap_halves(): other = lax.ppermute(half, 'req', pairs)]
    unnamed x13 -> x18, local copies, waits for them, and re-layouts: 7.11 us -> 3.82 us
  transfers between devices with their start and end apart: 3 -> 4, of which waited for: 3 -> 4; matrix products, arithmetic and copies ran while one was open for 4% -> 6% of each run, Pallas kernels for 0% -> 0%
where the time goes in v1:
time: 231 us; the launch traced here: 230 us
  Pallas kernels  146 us (63%)
  waiting for transfers between devices  40 us (17%)
  local copies, waits for them, and re-layouts  15.4 us (7%)
  other arithmetic  11.3 us (5%)
  matrix products  8.84 us (4%)
  starting transfers between devices  6.45 us (3%)
    pallas_call x1, Pallas kernels, mlp_fused(): pl.pallas_call(functools.partial(mlp_kernel, chips), out_shape=jax.ShapeD...  146 us
    ppermute x4, waiting for transfers between devices, swap_halves(): other = lax.ppermute(half, 'req', pairs)  40 us
    ppermute x4, starting transfers between devices, swap_halves(): other = lax.ppermute(half, 'req', pairs)  6.45 us
  transfers between devices with their start and end apart: 4, of which 4 were waited for; matrix products, arithmetic and copies ran while one was open for 6% of the time, Pallas kernels for 0%

profile of v1, /device:TPU:0, one launch (start us, length us, event | category | flops | bytes accessed | tf_op | source)
XLA Modules:
  0.0 230.3 jit_solution(11139584191950074057)
XLA Ops:
  0.0 3.1 %slice_bitcast_fusion = (bf16[128,4096]{1,0:T(8,128)(2,1)}, bf16[128,4096]{1,0:T(8,128)(2,1)}) fusion(bf16[1,1,2,128,4096]{4,3,2,1,0:T(8,128)(2,1)} %param.10), kind=kLoop, calls=%fused_computation.27 | loop fusion | bytes 4194304 | tf_op jit(solution)/shard_map/squeeze | solution.py:29
  3.1 3.0 %collective-permute-start = (bf16[128,4096]{1,0:T(8,128)(2,1)}, bf16[128,4096]{1,0:T(8,128)(2,1)}, u32[]{:S(2)}, u32[]{:S(2)}) collective-permute-start(bf16[128,4096]{1,0:T(8,128)(2,1)} %get-tuple-element.18), channel_id=1, source_target_pairs={{0,16},{8,24},{16,0},{24,8},{1,17},{9,25},{17,1},{25,9},{2,18},{10... | collective-permute-start | bytes 3145736 | tf_op jit(solution)/shard_map/ppermute | solution.py:21
  6.1 1.5 collective-permute-start.2
  9.7 2.2 fusion.22
  11.9 17.6 %collective-permute-done = bf16[128,4096]{1,0:T(8,128)(2,1)} collective-permute-done((bf16[128,4096]{1,0:T(8,128)(2,1)}, bf16[128,4096]{1,0:T(8,128)(2,1)}, u32[]{:S(2)}, u32[]{:S(2)}) %collective-permute-start) | collective-permute-done | bytes 1048608 | tf_op jit(solution)/shard_map/ppermute | solution.py:21
  29.6 1.5 collective-permute-done.2
  31.0 2.8 %broadcast_select_fusion.1 = (bf16[128,4096]{1,0:T(8,128)(2,1)}, bf16[128,4096]{1,0:T(8,128)(2,1)}) fusion(bf16[128,4096]{1,0:T(8,128)(2,1)} %collective-permute-done.2, pred[]{:T(512)S(6)} %eq.8, bf16[1,1,2,128,4096]{4,3,2,1,0:T(8,128)(2,1)S(1)} %copy-done, bf16[128,4096]{1,0:T(8,128)(2,1)} %collective-permute-done, pred[]{:T(512)S(6)} %eq.9), kind=kLoop, calls=%fused_computation.30 | loop fusion | flops 1048576 | bytes 6291458 | tf_op jit(solution)/shard_map/jit(_where)/select_n | solution.py:23
  34.1 1.3 copy.38
  35.4 1.3 copy.39
  37.4 1.6 copy.37
  39.8 2.3 %fusion.23 = (f32[32,128]{1,0:T(8,128)S(1)}, f32[32,128,128]{1,2,0:T(8,128)S(1)}) fusion(f32[128,128]{0,1:T(8,128)S(1)} %get-tuple-element.20, f32[32]{0:T(128)S(1)} %multiply_exponential_fusion, bf16[128,32,128]{0,2,1:T(8,128)(2,1)} %bitcast.72, bf16[128,32,128]{0,2,1:T(8,128)(2,1)} %bitcast.75, pred[128,128]{0,1:T(8,128)(4,1)S(1)} %broadcast_compare_fusion), kind=kOutput, calls=%fused_computation.48 | convolution fusion | flops 136835072 | bytes 4292736 | tf_op jit(solution)/shard_map/qhe,khe->hqk/dot_general | solution.py:40
  42.1 1.8 fusion.9
  43.9 1.7 collective-permute-start.3
  45.6 12.3 %collective-permute-done.1 = bf16[128,4096]{1,0:T(8,128)(2,1)} collective-permute-done((bf16[128,4096]{1,0:T(8,128)(2,1)}, bf16[128,4096]{1,0:T(8,128)(2,1)}, u32[]{:S(2)}, u32[]{:S(2)}) %collective-permute-start.1) | collective-permute-done | bytes 1048608 | tf_op jit(solution)/shard_map/ppermute | solution.py:21
  57.9 1.3 broadcast_select_fusion.2
  59.3 1.3 copy.35
  60.6 8.6 %collective-permute-done.3 = bf16[128,4096]{1,0:T(8,128)(2,1)} collective-permute-done((bf16[128,4096]{1,0:T(8,128)(2,1)}, bf16[128,4096]{1,0:T(8,128)(2,1)}, u32[]{:S(2)}, u32[]{:S(2)}) %collective-permute-start.3) | collective-permute-done | bytes 1048608 | tf_op jit(solution)/shard_map/ppermute | solution.py:21
  69.2 2.2 fusion.24
  73.6 2.5 %convert_reduce_fusion = (f32[128]{0:T(128)S(1)}, bf16[128,32,128]{0,2,1:T(8,128)(2,1)}, f32[128,32,128]{0,2,1:T(8,128)}) fusion(f32[128,32,128]{0,2,1:T(8,128)S(1)} %bitcast.70, f32[128,32]{0,1:T(8,128)S(1)} %get-tuple-element.9, f32[128,32]{0,1:T(8,128)S(1)} %get-tuple-element.11, f32[32,128,128]{1,2,0:T(8,128)S(1)} %copy-done.4, ...), kind=kOutput, calls=%fused_computation.1 | convolution fusion | flops 139460480 | bytes 10551808 | tf_op jit(solution)/shard_map/hqk,khe->qhe/dot_general | solution.py:49
  76.1 2.0 copy.36
  78.2 1.8 fusion.1
  80.0 1.8 multiply_convert_fusion
  81.8 146.1 %shard_map.82 = bf16[128,4096]{1,0:T(8,128)(2,1)} custom-call(bf16[128,4096]{1,0:T(8,128)(2,1)} %get-tuple-element.5.normed_hbm, bf16[128,4096]{1,0:T(8,128)(2,1)} %get-tuple-element.6.state_ref, bf16[1536,4096]{1,0:T(8,128)(2,1)} %up_hbm.1, bf16[1536,4096]{1,0:T(8,128)(2,1)} %down_hbm.1), custom_call_target="tpu_custom_call" | custom-call | flops 25769803776 | bytes 25165824 | tf_op jit(solution)/shard_map/pallas_call | solution.py:345
  227.9 2.3 %select_bitcast_fusion = bf16[1,1,128,4096]{3,2,1,0:T(8,128)(2,1)} fusion(bf16[128,4096]{1,0:T(8,128)(2,1)} %shard_map.82, pred[128]{0:T(512)(128)(4,1)S(1)} %iota_compare_fusion), kind=kLoop, calls=%fused_computation.23 | loop fusion | flops 524288 | bytes 2097280 | tf_op jit(solution)/shard_map/broadcast_in_dim | solution.py:424
  (28 shorter events, 4.0 us)
Async XLA Ops:
  0.0 7.7 %copy-start.7 = (s32[8]{0:T(128)S(1)}, s32[8]{0:T(128)}, u32[]{:S(2)}) copy-start(s32[8]{0:T(128)} %param.11) | copy-start | bytes 100
  3.1 26.4 %collective-permute-start = (bf16[128,4096]{1,0:T(8,128)(2,1)}, bf16[128,4096]{1,0:T(8,128)(2,1)}, u32[]{:S(2)}, u32[]{:S(2)}) collective-permute-start(bf16[128,4096]{1,0:T(8,128)(2,1)} %get-tuple-element.18), channel_id=1, source_target_pairs={{0,16},{8,24},{16,0},{24,8},{1,17},{9,25},{17,1},{25,9},{2,18},{10... | collective-permute-start | bytes 3145736 | tf_op jit(solution)/shard_map/ppermute | solution.py:21
  6.1 24.9 %collective-permute-start.2 = (bf16[128,4096]{1,0:T(8,128)(2,1)}, bf16[128,4096]{1,0:T(8,128)(2,1)}, u32[]{:S(2)}, u32[]{:S(2)}) collective-permute-start(bf16[128,4096]{1,0:T(8,128)(2,1)} %get-tuple-element.17), channel_id=1, source_target_pairs={{0,8},{8,0},{16,24},{24,16},{1,9},{9,1},{17,25},{25,17},{2,10},{10... | collective-permute-start | bytes 3145736 | tf_op jit(solution)/shard_map/ppermute | solution.py:21
  9.7 21.3 %copy-start = (bf16[1,1,2,128,4096]{4,3,2,1,0:T(8,128)(2,1)S(1)}, bf16[1,1,2,128,4096]{4,3,2,1,0:T(8,128)(2,1)}, u32[]{:S(2)}) copy-start(bf16[1,1,2,128,4096]{4,3,2,1,0:T(8,128)(2,1)} %param.10) | copy-start | bytes 6291460
  33.8 24.1 %collective-permute-start.1 = (bf16[128,4096]{1,0:T(8,128)(2,1)}, bf16[128,4096]{1,0:T(8,128)(2,1)}, u32[]{:S(2)}, u32[]{:S(2)}) collective-permute-start(bf16[128,4096]{1,0:T(8,128)(2,1)} %get-tuple-element.16), channel_id=1, source_target_pairs={{0,8},{8,0},{16,24},{24,16},{1,9},{9,1},{17,25},{25,17},{2,10},{10... | collective-permute-start | bytes 3145736 | tf_op jit(solution)/shard_map/ppermute | solution.py:21
  35.4 2.0 copy-start.1
  43.9 25.3 %collective-permute-start.3 = (bf16[128,4096]{1,0:T(8,128)(2,1)}, bf16[128,4096]{1,0:T(8,128)(2,1)}, u32[]{:S(2)}, u32[]{:S(2)}) collective-permute-start(bf16[128,4096]{1,0:T(8,128)(2,1)} %get-tuple-element.15), channel_id=1, source_target_pairs={{0,16},{8,24},{16,0},{24,8},{1,17},{9,25},{17,1},{25,9},{2,18},{10... | collective-permute-start | bytes 3145736 | tf_op jit(solution)/shard_map/ppermute | solution.py:21
  69.2 3.3 %copy-start.5 = (bf16[128,4096]{0,1:T(8,128)(2,1)S(1)}, bf16[128,4096]{0,1:T(8,128)(2,1)}, u32[]{:S(2)}) copy-start(bf16[128,4096]{0,1:T(8,128)(2,1)} %copy.35) | copy-start | bytes 3145732
  71.4 1.6 copy-start.3
  71.4 2.2 copy-start.4
  76.1 3.8 %copy-start.2 = (bf16[1,1,128,4096]{3,2,1,0:T(8,128)(2,1)S(1)}, bf16[1,1,128,4096]{3,2,1,0:T(8,128)(2,1)}, u32[]{:S(2)}) copy-start(bf16[1,1,128,4096]{3,2,1,0:T(8,128)(2,1)} %param.8) | copy-start | bytes 3145732
  76.1 3.8 %copy-start.6 = (f32[4096]{0:T(1024)S(1)}, f32[4096]{0:T(1024)}, u32[]{:S(2)}) copy-start(f32[4096]{0:T(1024)} %param.13) | copy-start | bytes 49156

commit v2 on v1

--- a/solution.py
+++ b/solution.py
@@ -70,21 +70,22 @@
 
 
 MESH = pl.DeviceIdType.MESH
-AG_PARTS = 2
+AG_PARTS = 4
 RS_PARTS = 4
 UP_TILE = 512
 DOWN_TILE = 512
 
 
-def mlp_kernel(
-    chips, normed_hbm, state_ref, up_hbm, down_hbm, out_ref,
-    xg, upv, dnv, hid, part, sib, line,
-    wsem, ag_recv, ag_send, sib_send, sib_recv, rs_send, rs_recv,
+def layer_kernel(
+    chips, owner_ref, slope_ref, gain_ref, residual_ref, proj_hbm, cache_hbm, up_hbm, down_hbm,
+    out_ref,
+    xg, upv, dnv, hid, part, sib, line, xn, values_two,
+    wsem, ag_recv, ag_send, sib_send, sib_recv, rs_send, rs_recv, swap_send, swap_recv,
 ):
     rows = xg.shape[2]
     width = xg.shape[3]
     units = upv.shape[0]
-    ag_rows = rows // AG_PARTS
+    ag_cols = width // AG_PARTS
     rs_rows = rows // RS_PARTS
     me = lax.axis_index("grp")
     z = me // 2
@@ -95,13 +96,31 @@
 
     up_copy = pltpu.make_async_copy(up_hbm, upv, wsem.at[0])
     down_copy = pltpu.make_async_copy(down_hbm, dnv, wsem.at[1])
-    own_copy = pltpu.make_async_copy(normed_hbm, xg.at[z, c], wsem.at[2])
-    own_copy.start()
-    up_copy.start()
-    down_copy.start()
+    queries, keys, values = part.at[0, 0], part.at[0, 1], part.at[1, 0]
+    keys_own, values_own = part.at[1, 1], part.at[2, 0]
+    keys_one, values_one, keys_two = part.at[2, 1], part.at[3, 0], part.at[3, 1]
+    loads = [
+        pltpu.make_async_copy(cache_hbm.at[0], keys_own, wsem.at[2]),
+        pltpu.make_async_copy(cache_hbm.at[1], values_own, wsem.at[3]),
+        pltpu.make_async_copy(proj_hbm.at[0], queries, wsem.at[4]),
+        pltpu.make_async_copy(proj_hbm.at[1], keys, wsem.at[5]),
+        pltpu.make_async_copy(proj_hbm.at[2], values, wsem.at[6]),
+    ]
+    for load in loads:
+        load.start()
+
+    r = lax.axis_index("req")
+    low_bit, high_bit = r % 2, r // 2
+    peer_low = r + 1 - 2 * low_bit
+    peer_high = r + 2 - 4 * high_bit
+    owner = owner_ref[me]
+    same_low = (owner % 2) == low_bit
+    same_high = (owner // 2) == high_bit
 
     barrier = pltpu.get_barrier_semaphore()
     pl.semaphore_signal(barrier, inc=1, device_id={"grp": twin}, device_id_type=MESH)
+    for peer in (peer_low, peer_high):
+        pl.semaphore_signal(barrier, inc=1, device_id={"req": peer}, device_id_type=MESH)
 
     @pl.when(has_left)
     def _():
@@ -113,16 +132,52 @@
 
     @pl.when(jnp.logical_and(has_left, has_right))
     def _():
-        pl.semaphore_wait(barrier, 3)
+        pl.semaphore_wait(barrier, 5)
 
     @pl.when(jnp.logical_not(jnp.logical_and(has_left, has_right)))
     def _():
-        pl.semaphore_wait(barrier, 2)
-
-    own_copy.wait()
+        pl.semaphore_wait(barrier, 4)
+
+    def swap_copy(kind, i):
+        cols = pl.ds(i * ag_cols, ag_cols)
+        src, dst, peer = (
+            (keys_own, keys_one, peer_low),
+            (values_own, values_one, peer_high),
+            (keys_one, keys_two, peer_high),
+            (values_one, values_two, peer_low),
+        )[kind]
+        return pltpu.make_async_remote_copy(
+            src_ref=src.at[:, cols], dst_ref=dst.at[:, cols],
+            send_sem=swap_send.at[kind, i], recv_sem=swap_recv.at[kind, i],
+            device_id={"req": peer}, device_id_type=MESH,
+        )
+
+    def swap_start(i):
+        swap_copy(0, i).start()
+        swap_copy(1, i).start()
+
+    def swap_relay(i):
+        cols = pl.ds(i * ag_cols, ag_cols)
+        swap_copy(0, i).wait_recv()
+        keys_one[:, cols] = lax.select(same_low, keys_own[:, cols], keys_one[:, cols])
+        swap_copy(2, i).start()
+        swap_copy(1, i).wait_recv()
+        values_one[:, cols] = lax.select(same_high, values_own[:, cols], values_one[:, cols])
+        swap_copy(3, i).start()
+        if i + 2 < AG_PARTS:
+            swap_start(i + 2)
+
+    loads[0].wait()
+    loads[1].wait()
+    swap_start(0)
+    swap_start(1)
+    for load in loads[2:]:
+        load.wait()
+    up_copy.start()
+    down_copy.start()
 
     def ag_copy(zb, cc, s, way, target):
-        piece = xg.at[zb, cc, pl.ds(s * ag_rows, ag_rows)]
+        piece = xg.at[zb, cc, :, pl.ds(s * ag_cols, ag_cols)]
         return pltpu.make_async_remote_copy(
             src_ref=piece, dst_ref=piece,
             send_sem=ag_send.at[way, zb, s], recv_sem=ag_recv.at[zb, cc, s],
@@ -144,7 +199,48 @@
             device_id={"grp": target}, device_id_type=MESH,
         )
 
+    query_at = lax.broadcasted_iota(jnp.int32, (rows, rows), 0)
+    key_at = lax.broadcasted_iota(jnp.int32, (rows, rows), 1)
+    offset = (key_at - query_at).astype(jnp.float32)
+    causal = key_at <= query_at
+    head_size = width // HEADS
+    scale = 1.0 / math.sqrt(head_size)
+    nt = (((1,), (1,)), ((), ()))
+
+    def attend_head(h, carry):
+        cols = pl.ds(pl.multiple_of(h * head_size, head_size), head_size)
+        slope = slope_ref[h]
+        query = queries[:, cols]
+        old_keys = lax.select(same_high, keys_one[:, cols], keys_two[:, cols])
+        old_values = lax.select(same_low, values_one[:, cols], values_two[:, cols])
+        old = lax.dot_general(query, old_keys, nt, preferred_element_type=jnp.float32)
+        new = lax.dot_general(query, keys[:, cols], nt, preferred_element_type=jnp.float32)
+        old = old * scale + slope * (offset - float(rows))
+        new = jnp.where(causal, new * scale + slope * offset, -jnp.inf)
+        top = jnp.maximum(
+            jnp.max(old, axis=1, keepdims=True), jnp.max(new, axis=1, keepdims=True)
+        )
+        old = jnp.exp(old - top)
+        new = jnp.exp(new - top)
+        total = jnp.sum(old, axis=1, keepdims=True) + jnp.sum(new, axis=1, keepdims=True)
+        context = jnp.dot(
+            old.astype(jnp.bfloat16), old_values, preferred_element_type=jnp.float32
+        ) + jnp.dot(
+            new.astype(jnp.bfloat16), values[:, cols], preferred_element_type=jnp.float32
+        )
+        state = residual_ref[:, cols].astype(jnp.float32) + context / total
+        xg[z, c, :, cols] = state.astype(jnp.bfloat16)
+        return carry
+
+    heads = HEADS // AG_PARTS
+    swap_relay(0)
     for s in range(AG_PARTS):
+        if s + 1 < AG_PARTS:
+            swap_relay(s + 1)
+        swap_copy(2, s).wait_recv()
+        swap_copy(3, s).wait_recv()
+        lax.fori_loop(s * heads, (s + 1) * heads, attend_head, 0, unroll=2)
+
         @pl.when(has_right)
         def _():
             ag_copy(z, c, s, 0, me + 2).start()
@@ -155,6 +251,9 @@
 
         ag_copy(z, c, s, 2, twin).start()
 
+    for s in range(AG_PARTS):
+        for kind in range(4):
+            swap_copy(kind, s).wait_send()
     up_copy.wait()
     down_copy.wait()
 
@@ -162,10 +261,22 @@
         for s in range(AG_PARTS):
             ag_copy(zb, 1 - c, s, 2, twin).wait_recv()
 
+        def norm_step(t, carry):
+            span = pl.ds(pl.multiple_of((t % (rows // 16)) * 16, 16), 16)
+            dest = pl.ds(pl.multiple_of(t * 16, 16), 16)
+            raw = xg[zb, t // (rows // 16), span, :].astype(jnp.float32)
+            center = raw - jnp.mean(raw, axis=1, keepdims=True)
+            spread = jnp.mean(center * center, axis=1, keepdims=True)
+            scaled = center * lax.rsqrt(spread + NORM_EPS) * gain_ref[...]
+            xn[dest, :] = scaled.astype(jnp.bfloat16)
+            return carry
+
+        lax.fori_loop(0, 2 * rows // 16, norm_step, 0)
+
         def up_step(j, carry):
             cols = pl.ds(pl.multiple_of(j * UP_TILE, UP_TILE), UP_TILE)
             pre = lax.dot_general(
-                xg[zb].reshape(2 * rows, width), upv[cols, :],
+                xn[...], upv[cols, :],
                 (((1,), (1,)), ((), ())), preferred_element_type=jnp.float32,
             )
             act = 0.5 * pre * (1.0 + lax.erf(pre * math.sqrt(0.5)))
@@ -290,7 +401,7 @@
             total = part[z, c, span].astype(jnp.float32) + sib[z, span].astype(jnp.float32)
             for slot in slots:
                 total = total + line[slot, span].astype(jnp.float32)
-            total = total + state_ref[span].astype(jnp.float32)
+            total = total + xg[z, c, span, :].astype(jnp.float32)
             out_ref[span] = total.astype(jnp.bfloat16)
 
         @pl.when(jnp.logical_and(has_left, has_right))
@@ -326,28 +437,34 @@
     lax.fori_loop(0, chips, drain, 0)
 
 
-def mlp_bytes(grp_size, rows, width, units):
+def layer_bytes(grp_size, rows, width, units):
     chips = grp_size // 2
-    blocks = 2 * chips + 2 * chips + chips + chips + 1 + 4
+    blocks = 2 * chips + 2 * chips + chips + chips + 1 + 5
     return 2 * width * (blocks * rows + 2 * units) + 4 * rows * units
 
 
 VMEM_LIMIT = 60 * 1024 * 1024
 
 
-def mlp_fused(grp_size, normed, states, up_weight, down_weight):
+def layer_fused(
+    grp_size, owner_req, norm_gain, residual, suffix_proj, prefix_cache, up_weight, down_weight
+):
     chips = grp_size // 2
-    rows, width = normed.shape
+    rows, width = residual.shape
     units = up_weight.shape[0]
     bf16 = jnp.bfloat16
     dma = pltpu.SemaphoreType.DMA
     total_rows = rows * grp_size
     return pl.pallas_call(
-        functools.partial(mlp_kernel, chips),
+        functools.partial(layer_kernel, chips),
         out_shape=jax.ShapeDtypeStruct((rows, width), bf16),
         in_specs=[
+            pl.BlockSpec(memory_space=pltpu.SMEM),
+            pl.BlockSpec(memory_space=pltpu.SMEM),
+            pl.BlockSpec(memory_space=pltpu.VMEM),
+            pl.BlockSpec(memory_space=pltpu.VMEM),
             pl.BlockSpec(memory_space=pl.ANY),
-            pl.BlockSpec(memory_space=pltpu.VMEM),
+            pl.BlockSpec(memory_space=pl.ANY),
             pl.BlockSpec(memory_space=pl.ANY),
             pl.BlockSpec(memory_space=pl.ANY),
         ],
@@ -360,13 +477,17 @@
             pltpu.VMEM((chips, 2, rows, width), bf16),
             pltpu.VMEM((chips, rows, width), bf16),
             pltpu.VMEM((chips + 1, rows, width), bf16),
-            dma((3,)),
+            pltpu.VMEM((2 * rows, width), bf16),
+            pltpu.VMEM((rows, width), bf16),
+            dma((7,)),
             dma((chips, 2, AG_PARTS)),
             dma((3, chips, AG_PARTS)),
             dma((chips,)),
             dma((chips,)),
             dma((chips, RS_PARTS)),
             dma((chips + 1, RS_PARTS)),
+            dma((4, AG_PARTS)),
+            dma((4, AG_PARTS)),
         ],
         compiler_params=pltpu.CompilerParams(
             collective_id=0, has_side_effects=True, vmem_limit_bytes=VMEM_LIMIT
@@ -376,7 +497,10 @@
             bytes_accessed=4 * units * width,
             transcendentals=total_rows * units,
         ),
-    )(normed, states, up_weight, down_weight)
+    )(
+        owner_req, head_slopes(HEADS), norm_gain[None, :], residual, suffix_proj, prefix_cache,
+        up_weight, down_weight,
+    )
 
 
 def mlp_plain(normed, states, up_weight, down_weight):
@@ -403,6 +527,14 @@
     prefix_count = prefix_cache.shape[3]
     head_count = HEADS
     head_size = feature_count // head_count
+    live = jnp.arange(slot_count, dtype=jnp.int32) < lengths[0, 0]
+    needed = layer_bytes(grp_size, slot_count, feature_count, up_weight.shape[0])
+    if req_size == 4 and grp_size == 8 and needed <= VMEM_LIMIT * 15 // 16:
+        combined = layer_fused(
+            grp_size, owner_req, norm_gain, residual[0, 0], suffix_proj[0, 0], prefix_cache[0, 0],
+            up_weight, down_weight,
+        )
+        return jnp.where(live[:, None], combined, jnp.zeros_like(combined))[None, None]
     block = suffix_proj[0, 0].reshape(3, slot_count, head_count, head_size)
     query_pos = prefix_count + jnp.arange(slot_count, dtype=jnp.int32)
     prefix_pos = jnp.arange(prefix_count, dtype=jnp.int32)
@@ -415,11 +547,7 @@
     context = merge_parts(first, second)
     states = (residual[0, 0].astype(jnp.float32) + context).astype(jnp.bfloat16)
     normed = layer_norm(states, norm_gain)
-    if mlp_bytes(grp_size, slot_count, feature_count, up_weight.shape[0]) <= VMEM_LIMIT * 15 // 16:
-        combined = mlp_fused(grp_size, normed, states, up_weight, down_weight)
-    else:
-        combined = mlp_plain(normed, states, up_weight, down_weight)
-    live = jnp.arange(slot_count, dtype=jnp.int32) < lengths[0, 0]
+    combined = mlp_plain(normed, states, up_weight, down_weight)
     output = jnp.where(live[:, None], combined, jnp.zeros_like(combined))
     return output[None, None]
 

time: 231 us -> 205 us (0.89)
  Pallas kernels: 146 us -> 201 us
  waiting for transfers between devices: 40 us -> 0 us
  local copies, waits for them, and re-layouts: 15.4 us -> 0 us
  matrix products: 8.84 us -> 0 us
  other arithmetic: 11.3 us -> 2.87 us
  starting transfers between devices: 6.45 us -> 0 us
    pallas_call x1, Pallas kernels: 146 us -> 201 us  [layer_fused(): pl.pallas_call(functools.partial(layer_kernel, chips), out_shape=jax.Shap...]
    ppermute x4 -> x0, waiting for transfers between devices: 40 us -> none  [swap_halves(): other = lax.ppermute(half, 'req', pairs)]
    dot_general x4 -> x0, matrix products: 8.84 us -> none  [the longest x2 4.55 us: attend(): jnp.einsum('qhe,khe->hqk', queries, key_rows, preferred_element_type=jnp....]
    ppermute x4 -> x0, starting transfers between devices: 6.45 us -> none  [swap_halves(): other = lax.ppermute(half, 'req', pairs)]
    select_n x2 -> x0, other arithmetic: 4.16 us -> none  [swap_halves(): half = jnp.where(same, half, other)]
    unnamed x18 -> x0, local copies, waits for them, and re-layouts: 3.82 us -> none
    reshape x2 -> x0, local copies, waits for them, and re-layouts: 3.32 us -> none  [the longest x1 2.01 us: merge_parts(): return merged.reshape(merged.shape[0], merged.shape[1] * merged.shape[2])]
    squeeze x1 -> x0, local copies, waits for them, and re-layouts: 3.11 us -> none  [from_owner(): keys = swap_halves(block[0], bits, req_size, owner_index)]
  transfers between devices with their start and end apart: 4 -> 0, of which waited for: 4 -> 0; matrix products, arithmetic and copies ran while one was open for 6% -> 0% of each run, Pallas kernels for 0% -> 0%
where the time goes in v2:
time: 205 us; the launch traced here: 204 us
  Pallas kernels  201 us (98%)
  other arithmetic  2.87 us (1%)
    pallas_call x1, Pallas kernels, layer_fused(): pl.pallas_call(functools.partial(layer_kernel, chips), out_shape=jax.Shap...  201 us

profile of v2, /device:TPU:0, one launch (start us, length us, event | category | flops | bytes accessed | tf_op | source)
XLA Modules:
  0.0 204.4 jit_solution(5418630956022225607)
XLA Ops:
  0.7 0.5 multiply_exponential_fusion.slope_ref
  1.2 200.9 %shard_map.82 = bf16[128,4096]{1,0:T(8,128)(2,1)} custom-call(s32[8]{0:T(128)} %owner_ref.1, f32[32]{0:T(128)} %multiply_exponential_fusion.slope_ref, f32[1,4096]{1,0:T(1,128)} %bitcast.11, bf16[128,4096]{1,0:T(8,128)(2,1)} %bitcast.10, bf16[3,128,4096]{2,1,0:T(8,128)(2,1)} %bitcast.8, bf16[2,128,4096]{2,1,0:T(8,128)(2,1)} %bitcast.9, ...), custom_call_target="tpu_custom_call" | custom-call | flops 25769803776 | bytes 25165824 | tf_op jit(solution)/shard_map/pallas_call | solution.py:458
  202.1 2.3 %select_bitcast_fusion = bf16[1,1,128,4096]{3,2,1,0:T(8,128)(2,1)} fusion(bf16[128,4096]{1,0:T(8,128)(2,1)} %shard_map.82, pred[128]{0:T(512)(128)(4,1)S(1)} %iota_compare_fusion), kind=kLoop, calls=%fused_computation | loop fusion | flops 524288 | bytes 2097280 | tf_op jit(solution)/shard_map/broadcast_in_dim | solution.py:537
  (1 shorter events, 0.0 us)

commit v3 on v2

--- a/solution.py
+++ b/solution.py
@@ -199,6 +199,32 @@
             device_id={"grp": target}, device_id_type=MESH,
         )
 
+    def forward(t):
+        for d in range(1, chips):
+            s = t - d
+            if not 0 <= s < AG_PARTS:
+                continue
+
+            @pl.when(z - d >= 0)
+            def _():
+                ag_copy(z - d, c, s, 0, twin).wait_recv()
+
+                @pl.when(has_right)
+                def _():
+                    ag_copy(z - d, c, s, 0, me + 2).start()
+
+                ag_copy(z - d, c, s, 2, twin).start()
+
+            @pl.when(z + d < chips)
+            def _():
+                ag_copy(z + d, c, s, 1, twin).wait_recv()
+
+                @pl.when(has_left)
+                def _():
+                    ag_copy(z + d, c, s, 1, me - 2).start()
+
+                ag_copy(z + d, c, s, 2, twin).start()
+
     query_at = lax.broadcasted_iota(jnp.int32, (rows, rows), 0)
     key_at = lax.broadcasted_iota(jnp.int32, (rows, rows), 1)
     offset = (key_at - query_at).astype(jnp.float32)
@@ -239,7 +265,7 @@
             swap_relay(s + 1)
         swap_copy(2, s).wait_recv()
         swap_copy(3, s).wait_recv()
-        lax.fori_loop(s * heads, (s + 1) * heads, attend_head, 0, unroll=2)
+        lax.fori_loop(s * heads, (s + 1) * heads, attend_head, 0, unroll=4)
 
         @pl.when(has_right)
         def _():
@@ -250,6 +276,7 @@
             ag_copy(z, c, s, 1, me - 2).start()
 
         ag_copy(z, c, s, 2, twin).start()
+        forward(s)
 
     for s in range(AG_PARTS):
         for kind in range(4):
@@ -302,32 +329,20 @@
         part[zb, c, span] = total.astype(jnp.bfloat16)
 
     def step(d, carry):
-        low, high = z - d, z + d
-        for s in range(AG_PARTS):
-            @pl.when(jnp.logical_and(d > 0, low >= 0))
-            def _():
-                ag_copy(low, c, s, 0, twin).wait_recv()
-
-                @pl.when(has_right)
-                def _():
-                    ag_copy(low, c, s, 0, me + 2).start()
-
-                ag_copy(low, c, s, 2, twin).start()
-
-            @pl.when(jnp.logical_and(d > 0, high < chips))
-            def _():
-                ag_copy(high, c, s, 1, twin).wait_recv()
-
-                @pl.when(has_left)
-                def _():
-                    ag_copy(high, c, s, 1, me - 2).start()
-
-                ag_copy(high, c, s, 2, twin).start()
+        inward = jnp.where(z < chips // 2, 1, -1)
+        is_end = jnp.logical_or(z == 0, z == chips - 1)
 
         def side_step(side, inner):
-            zb = z - d + 2 * d * side
-
-            @pl.when(jnp.logical_and(jnp.logical_and(zb >= 0, zb < chips), d + 1 > side))
+            place = 2 * (d - 1) + side
+            for at, t in ((0, AG_PARTS), (1, AG_PARTS + 1), (3, AG_PARTS + 2)):
+                @pl.when(place == at)
+                def _():
+                    forward(t)
+
+            own = jnp.logical_and(side == 1, d == jnp.where(is_end, chips, chips - 1))
+            zb = jnp.where(own, z, z + inward * d * (1 - 2 * side))
+
+            @pl.when(jnp.logical_and(zb >= 0, zb < chips))
             def _():
                 compute(zb)
 
@@ -337,8 +352,8 @@
 
         to_right = d
         to_left = chips - 1 - d
-        goes_right = z < to_right
-        goes_left = z > to_left
+        goes_right = jnp.logical_and(z < to_right, d < chips)
+        goes_left = jnp.logical_and(z > to_left, d < chips)
 
         @pl.when(goes_right)
         def _():
@@ -383,7 +398,7 @@
 
         return carry
 
-    lax.fori_loop(0, chips, step, 0)
+    lax.fori_loop(1, chips + 1, step, 0)
 
     sib_copy(z).wait_recv()
     for q in range(RS_PARTS):

time: 205 us -> 225 us (1.098)
  Pallas kernels: 201 us -> 221 us
    pallas_call x1, Pallas kernels: 201 us -> 221 us  [layer_fused(): pl.pallas_call(functools.partial(layer_kernel, chips), out_shape=jax.Shap...]
where the time goes in v3:
time: 225 us; the launch traced here: 224 us
  Pallas kernels  221 us (98%)
  other arithmetic  2.87 us (1%)
    pallas_call x1, Pallas kernels, layer_fused(): pl.pallas_call(functools.partial(layer_kernel, chips), out_shape=jax.Shap...  221 us

profile of v3, /device:TPU:0, one launch (start us, length us, event | category | flops | bytes accessed | tf_op | source)
XLA Modules:
  0.0 224.5 jit_solution(5259421437547278271)
XLA Ops:
  0.7 0.5 multiply_exponential_fusion.slope_ref
  1.2 220.9 %shard_map.82 = bf16[128,4096]{1,0:T(8,128)(2,1)} custom-call(s32[8]{0:T(128)} %owner_ref.1, f32[32]{0:T(128)} %multiply_exponential_fusion.slope_ref, f32[1,4096]{1,0:T(1,128)} %bitcast.11, bf16[128,4096]{1,0:T(8,128)(2,1)} %bitcast.10, bf16[3,128,4096]{2,1,0:T(8,128)(2,1)} %bitcast.8, bf16[2,128,4096]{2,1,0:T(8,128)(2,1)} %bitcast.9, ...), custom_call_target="tpu_custom_call" | custom-call | flops 25769803776 | bytes 25165824 | tf_op jit(solution)/shard_map/pallas_call | solution.py:473
  222.1 2.3 %select_bitcast_fusion = bf16[1,1,128,4096]{3,2,1,0:T(8,128)(2,1)} fusion(bf16[128,4096]{1,0:T(8,128)(2,1)} %shard_map.82, pred[128]{0:T(512)(128)(4,1)S(1)} %iota_compare_fusion), kind=kLoop, calls=%fused_computation | loop fusion | flops 524288 | bytes 2097280 | tf_op jit(solution)/shard_map/broadcast_in_dim | solution.py:552
  (1 shorter events, 0.0 us)

commit v4 on v3

--- a/solution.py
+++ b/solution.py
@@ -79,7 +79,7 @@
 def layer_kernel(
     chips, owner_ref, slope_ref, gain_ref, residual_ref, proj_hbm, cache_hbm, up_hbm, down_hbm,
     out_ref,
-    xg, upv, dnv, hid, part, sib, line, xn, values_two,
+    xg, upv, dnv, hid, part, sib, line, xn, xt, values_two,
     wsem, ag_recv, ag_send, sib_send, sib_recv, rs_send, rs_recv, swap_send, swap_recv,
 ):
     rows = xg.shape[2]
@@ -265,7 +265,7 @@
             swap_relay(s + 1)
         swap_copy(2, s).wait_recv()
         swap_copy(3, s).wait_recv()
-        lax.fori_loop(s * heads, (s + 1) * heads, attend_head, 0, unroll=4)
+        lax.fori_loop(s * heads, (s + 1) * heads, attend_head, 0, unroll=2)
 
         @pl.when(has_right)
         def _():
@@ -300,14 +300,18 @@
 
         lax.fori_loop(0, 2 * rows // 16, norm_step, 0)
 
+        def turn_step(j, carry):
+            cols = pl.ds(pl.multiple_of(j * UP_TILE, UP_TILE), UP_TILE)
+            xt[cols, :] = xn[:, cols].T
+            return carry
+
+        lax.fori_loop(0, width // UP_TILE, turn_step, 0)
+
         def up_step(j, carry):
             cols = pl.ds(pl.multiple_of(j * UP_TILE, UP_TILE), UP_TILE)
-            pre = lax.dot_general(
-                xn[...], upv[cols, :],
-                (((1,), (1,)), ((), ())), preferred_element_type=jnp.float32,
-            )
+            pre = jnp.dot(upv[cols, :], xt[...], preferred_element_type=jnp.float32)
             act = 0.5 * pre * (1.0 + lax.erf(pre * math.sqrt(0.5)))
-            hid[:, cols] = act.astype(jnp.bfloat16)
+            hid[:, cols] = act.astype(jnp.bfloat16).T
             return carry
 
         lax.fori_loop(0, units // UP_TILE, up_step, 0)
@@ -454,7 +458,7 @@
 
 def layer_bytes(grp_size, rows, width, units):
     chips = grp_size // 2
-    blocks = 2 * chips + 2 * chips + chips + chips + 1 + 5
+    blocks = 2 * chips + 2 * chips + chips + chips + 1 + 7
     return 2 * width * (blocks * rows + 2 * units) + 4 * rows * units
 
 
@@ -493,6 +497,7 @@
             pltpu.VMEM((chips, rows, width), bf16),
             pltpu.VMEM((chips + 1, rows, width), bf16),
             pltpu.VMEM((2 * rows, width), bf16),
+            pltpu.VMEM((width, 2 * rows), bf16),
             pltpu.VMEM((rows, width), bf16),
             dma((7,)),
             dma((chips, 2, AG_PARTS)),
@@ -544,7 +549,7 @@
     head_size = feature_count // head_count
     live = jnp.arange(slot_count, dtype=jnp.int32) < lengths[0, 0]
     needed = layer_bytes(grp_size, slot_count, feature_count, up_weight.shape[0])
-    if req_size == 4 and grp_size == 8 and needed <= VMEM_LIMIT * 15 // 16:
+    if req_size == 4 and grp_size == 8 and needed <= VMEM_LIMIT:
         combined = layer_fused(
             grp_size, owner_req, norm_gain, residual[0, 0], suffix_proj[0, 0], prefix_cache[0, 0],
             up_weight, down_weight,

time: 225 us -> 227 us (level)
    pallas_call x1, Pallas kernels: 221 us -> 223 us  [layer_fused(): pl.pallas_call(functools.partial(layer_kernel, chips), out_shape=jax.Shap...]
where the time goes in v4:
time: 227 us
  Pallas kernels  223 us (98%)
  other arithmetic  2.87 us (1%)
    pallas_call x1, Pallas kernels, layer_fused(): pl.pallas_call(functools.partial(layer_kernel, chips), out_shape=jax.Shap...  223 us

profile of v4, /device:TPU:0, one launch (start us, length us, event | category | flops | bytes accessed | tf_op | source)
XLA Modules:
  0.0 226.7 jit_solution(2445687951114680567)
XLA Ops:
  0.7 0.5 multiply_exponential_fusion.slope_ref
  1.2 223.2 %shard_map.82 = bf16[128,4096]{1,0:T(8,128)(2,1)} custom-call(s32[8]{0:T(128)} %owner_ref.1, f32[32]{0:T(128)} %multiply_exponential_fusion.slope_ref, f32[1,4096]{1,0:T(1,128)} %bitcast.11, bf16[128,4096]{1,0:T(8,128)(2,1)} %bitcast.10, bf16[3,128,4096]{2,1,0:T(8,128)(2,1)} %bitcast.8, bf16[2,128,4096]{2,1,0:T(8,128)(2,1)} %bitcast.9, ...), custom_call_target="tpu_custom_call" | custom-call | flops 25769803776 | bytes 25165824 | tf_op jit(solution)/shard_map/pallas_call | solution.py:477
  224.4 2.3 %select_bitcast_fusion = bf16[1,1,128,4096]{3,2,1,0:T(8,128)(2,1)} fusion(bf16[128,4096]{1,0:T(8,128)(2,1)} %shard_map.82, pred[128]{0:T(512)(128)(4,1)S(1)} %iota_compare_fusion), kind=kLoop, calls=%fused_computation | loop fusion | flops 524288 | bytes 2097280 | tf_op jit(solution)/shard_map/broadcast_in_dim | solution.py:557
  (1 shorter events, 0.0 us)
